TPU v7x, 256 devices: a whole 4x4x8 slice. The times are simulated.
256 devices in a mesh: row: 8 (over x, y_hi), col: 32 (over y_lo, z, core).
Axes of the slice: x: 4, y: 4 (y_hi: 2, y_lo: 2; y = y_hi * 2 + y_lo), z: 8, core: 2. Of those that a mesh axis runs over, the one named last changes fastest.
Arguments:
- x_blocks: float32 [8, 128, 128, 128], P('row', 'col'), may hold values from -0.5 to 0.5
- x_rows: int32 [8, 128], P('row', 'col'), may hold values from 0 to 75, as said below
- x_cols: int32 [8, 128], P('row', 'col'), may hold values from 0 to 18, as said below
- y_blocks: float32 [608, 32, 128, 128], P('row', 'col'), may hold values from -6 to 6
- y_cols: int32 [608, 32], P('row', 'col'), may hold values from 0 to 18, as said below
- z_rows: int32 [8, 1280], P('row', 'col'), may hold values from 0 to 75, as said below
- z_cols: int32 [8, 1280], P('row', 'col'), may hold values from 0 to 18, as said below
Outputs:
- z_blocks: float32 [8, 1280, 128, 128], P('row', 'col')
Inputs may be any that keep to these rules, and one draw needn't show every extreme that they name: `x_rows`: position of a stored block of X inside its grid cell of 76 block rows; positions may repeat. `x_cols`: position of a stored block of X inside its grid cell of 19 block columns. `y_cols`: position of a stored block of Y inside its column cell of 19 block columns. `z_rows`: every retained position of the product receives at least one product of a stored block of X with a stored block of Y; positions may repeat. `z_cols`: column position of a retained product block inside its cell.
All inputs are finite; a program needn't handle non-finite values.
Results may differ from a plain program's by a relative error of at most 0.0003.
Values sent between devices are 32-bit elements; how exact they have to be, the bound alone decides.
No kernel may reach another device: no remote copies, remote signals or barrier semaphores. Data moves between devices by JAX's collectives and lax.ppermute only.
A program may use at most 128 MiB of HBM per device.

v0:
```python
import jax
import jax.numpy as jnp
from jax import lax
from jax.sharding import PartitionSpec as P


def local(x_blocks, x_rows, x_cols, y_blocks, y_cols, z_rows, z_cols):
    rows_count = lax.axis_size("row")
    cols_count = lax.axis_size("col")
    cell_ratio = cols_count // rows_count
    block_edge = x_blocks.shape[-1]
    per_cell = x_blocks.shape[1]
    targets = z_rows.shape[1]
    panel_rows = y_blocks.shape[0]
    stored_per_row = y_blocks.shape[1]
    cell_width = panel_rows // cell_ratio
    group_size = cell_ratio * per_cell
    whole_blocks, whole_rows, whole_cols = (
        lax.all_gather(x_blocks, "col", axis=1, tiled=True),
        lax.all_gather(x_rows, "col", axis=1, tiled=True),
        lax.all_gather(x_cols, "col", axis=1, tiled=True),
    )
    sorted_blocks = whole_blocks.reshape(rows_count, group_size, block_edge, block_edge)
    sorted_rows = whole_rows.reshape(rows_count, group_size)
    sorted_cols = whole_cols.reshape(rows_count, group_size)
    got_blocks, got_rows, got_cols = (
        lax.all_to_all(sorted_blocks, "row", split_axis=0, concat_axis=0, tiled=True),
        lax.all_to_all(sorted_rows, "row", split_axis=0, concat_axis=0, tiled=True),
        lax.all_to_all(sorted_cols, "row", split_axis=0, concat_axis=0, tiled=True),
    )
    want_rows, want_cols = (
        lax.all_gather(z_rows, "row", axis=0, tiled=True),
        lax.all_gather(z_cols, "row", axis=0, tiled=True),
    )
    slot_total = rows_count * group_size
    cell_offset = jnp.arange(group_size, dtype=jnp.int32) // per_cell * cell_width
    local_inner = (got_cols + cell_offset[None, :]).reshape(slot_total)
    anchor = jnp.broadcast_to(
        jnp.arange(rows_count, dtype=jnp.int32)[:, None], (rows_count, group_size)
    ).reshape(slot_total)
    left_blocks = got_blocks.reshape(slot_total, block_edge, block_edge)
    right_blocks = jnp.take(y_blocks, local_inner, axis=0)
    right_cols = jnp.take(y_cols, local_inner, axis=0)
    products = jnp.einsum(
        "mxy,mtyz->mtxz", left_blocks, right_blocks, precision=lax.Precision.HIGHEST
    )
    stacked = products.reshape(slot_total * stored_per_row, block_edge * block_edge)
    product_codes = (
        (anchor[:, None] * panel_rows + got_rows.reshape(slot_total)[:, None]) * cell_width
        + right_cols
    ).reshape(slot_total * stored_per_row)
    target_codes = (
        (jnp.arange(rows_count, dtype=jnp.int32)[:, None] * panel_rows + want_rows) * cell_width
        + want_cols
    ).reshape(rows_count * targets)
    matches = (target_codes[:, None] == product_codes[None, :]).astype(jnp.float32)
    summed = jnp.dot(matches, stacked, precision=lax.Precision.HIGHEST)
    own_blocks = lax.psum_scatter(
        summed.reshape(targets * lax.axis_size("row"), block_edge, block_edge),
        "row",
        scatter_dimension=0,
        tiled=True,
    )
    return own_blocks[None]


def solution(mesh):
    placed = (
        P("row", "col", None, None),
        P("row", "col"),
        P("row", "col"),
        P("row", "col", None, None),
        P("row", "col"),
        P("row", "col"),
        P("row", "col"),
    )
    return jax.shard_map(
        local, mesh=mesh, in_specs=placed, out_specs=P("row", "col", None, None), check_vma=False
    )
```

profile of v0, /device:TPU:2, one launch (start us, length us, event | category | flops | bytes accessed | tf_op | source)
XLA Modules:
  0.0 535.4 jit_solution(11020606725802298560)
XLA Ops:
  6.5 0.0 copy-start
  6.5 0.0 all-gather.4.cloned.1.call-start
  6.5 0.7 all-gather.4.cloned.1.call-update
  7.3 1.3 dynamic-slice
  9.2 0.8 bitcast_dynamic-update-slice_fusion
  9.9 0.7 bitcast_dynamic-update-slice_fusion.1
  10.7 19.5 %all-reduce.2 = (s32[128]{0:T(128)S(1)}, s32[128]{0:T(128)S(1)}) all-reduce(s32[128]{0:T(128)S(1)} %bitcast_dynamic-update-slice_fusion, s32[128]{0:T(128)S(1)} %bitcast_dynamic-update-slice_fusion.1), channel_id=1, replica_groups=mesh['row'=8,'col'=32] {'col'}, use_global_device_ids=true, to_apply=%add.1 | all-reduce | flops 256 | bytes 2048
  30.1 0.7 all_to_all.19
  30.8 7.2 %all-to-all-start = ((s32[8,1,16]{2,1,0:T(1,128)}), s32[8,1,16]{2,1,0:T(1,128)S(1)}, u32[]{:S(2)}, u32[]{:S(2)}) async-start(s32[8,1,16]{2,1,0:T(1,128)} %bitcast.6), calls=%async_computation | async-start | bytes 8192 | tf_op jit(solution)/shard_map/all_to_all | solution.py:28
  38.0 0.1 all_to_all.21
  38.1 6.0 %all-to-all-done = s32[8,1,16]{2,1,0:T(1,128)S(1)} async-done(((s32[8,1,16]{2,1,0:T(1,128)}), s32[8,1,16]{2,1,0:T(1,128)S(1)}, u32[]{:S(2)}, u32[]{:S(2)}) %all-to-all-start) | async-done | bytes 544 | tf_op jit(solution)/shard_map/all_to_all | solution.py:28
  44.1 10.0 %all_to_all.29 = s32[8,1,16]{2,1,0:T(1,128)S(1)} all-to-all(s32[8,1,16]{2,1,0:T(1,128)S(1)} %bitcast.43), channel_id=1, replica_groups=mesh['row'=8,'col'=32] {'row'}, dimensions={0} | all-to-all | bytes 1024 | tf_op jit(solution)/shard_map/all_to_all | solution.py:29
  54.1 30.4 %all-gather.4.cloned.1.call-done = f32[1,128,128,128]{3,2,0,1:T(8,128)} async-done(((f32[1,4,128,128]{3,2,0,1:T(8,128)}), f32[1,128,128,128]{3,2,0,1:T(8,128)}) %all-gather.4.cloned.1.call-update) | async-done | bytes 8388624 | tf_op jit(solution)/shard_map/all_gather | solution.py:19
  84.5 0.0 copy-start.2
  84.5 0.0 copy-start.3
  84.5 7.3 %all-to-all-start.2 = ((f32[8,16,128,128]{3,2,1,0:T(8,128)}), f32[8,16,128,128]{3,2,1,0:T(8,128)}, u32[]{:S(2)}, u32[]{:S(2)}) async-start(f32[8,16,128,128]{3,2,1,0:T(8,128)} %bitcast.37), calls=%async_computation.2 | async-start | bytes 16777216 | tf_op jit(solution)/shard_map/all_to_all | solution.py:27
  91.8 0.0 reduce-scatter.2.cloned.1.call-start
  91.8 0.1 add.105
  91.9 0.1 add.102
  92.0 0.0 copy-done.2
  92.0 126.4 %all-gather = s32[8,1,40]{2,1,0:T(1,128)S(1)} all-gather(s32[1,1,40]{2,1,0:T(1,128)S(1)} %bitcast.44), channel_id=1, replica_groups=mesh['row'=8,'col'=32] {'row'}, dimensions={0}, use_global_device_ids=true | all-gather | bytes 1440 | tf_op jit(solution)/shard_map/all_gather | solution.py:32
  218.4 0.0 copy-done.3
  218.4 19.2 %all-gather.1 = s32[8,1,40]{2,1,0:T(1,128)S(1)} all-gather(s32[1,1,40]{2,1,0:T(1,128)S(1)} %bitcast.45), channel_id=1, replica_groups=mesh['row'=8,'col'=32] {'row'}, dimensions={0}, use_global_device_ids=true | all-gather | bytes 1440 | tf_op jit(solution)/shard_map/all_gather | solution.py:33
  237.6 0.1 multiply_add_fusion
  237.7 0.1 eq.15
  237.8 0.1 mul.57
  237.8 0.5 broadcast.144
  238.4 0.7 reduce.9
  239.0 0.1 broadcast_in_dim_reshape.2
  239.1 0.1 all_to_all.24
  239.2 0.7 reduce.8
  239.9 0.1 all_to_all.23
  240.0 0.0 copy-done
  240.0 1.2 gather_fusion
  241.2 6.7 %gather_fusion.1 = f32[128,128,128]{2,1,0:T(8,128)} fusion(f32[76,128,128]{2,1,0:T(8,128)} %bitcast.36, s32[1024]{0:T(1024)S(1)} %pad_clamp_fusion), kind=kCustom, calls=%fused_computation.1 | custom fusion | bytes 16777728 | tf_op jit(solution)/shard_map/jit(_take)/gather | solution.py:42
  247.9 0.0 all-to-all-done.2
  247.9 21.3 %fusion.6 = f32[128,1,128,128]{2,3,0,1:T(8,128)} fusion(f32[128,128,128]{2,1,0:T(8,128)} %bitcast.15, f32[128,128,128]{2,1,0:T(8,128)} %gather_fusion.1, pred[128]{0:T(512)(128)(4,1)S(1)} %get-tuple-element.8), kind=kOutput, calls=%fused_computation.8 | convolution fusion | flops 3223322624 | bytes 25165952 | tf_op jit(solution)/shard_map/mxy,mtyz->mtxz/dot_general | solution.py:44
  269.2 9.4 %copy.19 = f32[128,1,128,128]{0,3,2,1:T(8,128)} copy(f32[128,1,128,128]{2,3,0,1:T(8,128)} %fusion.6) | data formatting | bytes 16777216 | tf_op jit(solution)/shard_map/mxy,mtyz->mtxz/transpose | solution.py:44
  278.6 17.0 %fusion = f32[320,128,128]{2,0,1:T(8,128)} fusion(f32[128,1,128,128]{0,3,2,1:T(8,128)} %copy.19, s32[128]{0:T(128)S(1)} %get-tuple-element.7, s32[320]{0:T(512)S(1)} %eq.15), kind=kOutput, calls=%fused_computation.2 | convolution fusion | flops 8053104640 | bytes 29361920 | tf_op jit(solution)/shard_map/dot_general | solution.py:57
  295.7 0.0 copy-start.1
  295.7 0.0 reduce-scatter.2.cloned.1.call-update
  295.7 229.1 %reduce-scatter.2.cloned.1.call-done = f32[40,128,128]{2,0,1:T(8,128)} async-done(((f32[320,128,128]{2,0,1:T(8,128)}), f32[40,128,128]{2,0,1:T(8,128)}) %reduce-scatter.2.cloned.1.call-update) | async-done | bytes 2621456 | tf_op jit(solution)/shard_map/reduce_scatter | solution.py:58
  524.8 3.7 copy.20
  528.6 0.0 copy-done.1
  (9 shorter events, 0.0 us)
Async XLA Ops:
  6.5 233.4 %copy-start = (s32[76,1]{0,1:T(1,128)S(1)}, s32[76,1]{0,1:T(1,128)}, u32[]{:S(2)}) copy-start(s32[76,1]{0,1:T(1,128)} %param.11) | copy-start | bytes 916
  6.5 77.9 %all-gather.4.cloned.1.call-start = ((), (), s32[]{:S(2)}) async-start(), calls=%async_computation.4 | async-start | bytes 8650752 | tf_op jit(solution)/shard_map/all_gather | solution.py:19
  30.8 13.3 %all-to-all-start = ((s32[8,1,16]{2,1,0:T(1,128)}), s32[8,1,16]{2,1,0:T(1,128)S(1)}, u32[]{:S(2)}, u32[]{:S(2)}) async-start(s32[8,1,16]{2,1,0:T(1,128)} %bitcast.6), calls=%async_computation | async-start | bytes 8192 | tf_op jit(solution)/shard_map/all_to_all | solution.py:28
  84.5 7.5 %copy-start.2 = (s32[1,40]{1,0:T(1,128)S(1)}, s32[1,40]{1,0:T(1,128)}, u32[]{:S(2)}) copy-start(s32[1,40]{1,0:T(1,128)} %param.12) | copy-start | bytes 484
  84.5 133.9 %copy-start.3 = (s32[1,40]{1,0:T(1,128)S(1)}, s32[1,40]{1,0:T(1,128)}, u32[]{:S(2)}) copy-start(s32[1,40]{1,0:T(1,128)} %param.13) | copy-start | bytes 484
  84.5 163.4 %all-to-all-start.2 = ((f32[8,16,128,128]{3,2,1,0:T(8,128)}), f32[8,16,128,128]{3,2,1,0:T(8,128)}, u32[]{:S(2)}, u32[]{:S(2)}) async-start(f32[8,16,128,128]{3,2,1,0:T(8,128)} %bitcast.37), calls=%async_computation.2 | async-start | bytes 16777216 | tf_op jit(solution)/shard_map/all_to_all | solution.py:27
  91.8 433.0 %reduce-scatter.2.cloned.1.call-start = ((), (), s32[]{:S(2)}) async-start(), calls=%async_computation.5 | async-start | bytes 23592960 | tf_op jit(solution)/shard_map/reduce_scatter | solution.py:58
  295.7 232.9 %copy-start.1 = (s32[76,1]{0,1:T(1,128)S(1)}, s32[76,1]{0,1:T(1,128)}, u32[]{:S(2)}) copy-start(s32[76,1]{0,1:T(1,128)} %param.11) | copy-start | bytes 916
Sparse Core Ops, SparseCore 0:
  9.2 75.2 all-gather.3
  295.8 228.9 reduce-scatter.1
where the time goes:
time: 537 us; the launch traced here: 535 us
  waiting for transfers between devices  266 us (50%)
  blocking collectives  175 us (33%)
  matrix products  38.3 us (7%)
  local copies, waits for them, and re-layouts  25.7 us (5%)
  starting transfers between devices  14.5 us (3%)
  between operations  14.1 us (3%)
    reduce_scatter x1, waiting for transfers between devices, local(): lax.psum_scatter(summed.reshape(targets * lax.axis_size('row'), block_edg...  229 us
    all_gather x1, blocking collectives, local(): lax.all_gather(z_rows, 'row', axis=0, tiled=True)  126 us
    all_gather x1, waiting for transfers between devices, local(): lax.all_gather(x_blocks, 'col', axis=1, tiled=True)  30.4 us
    dot_general x1, matrix products, local(): jnp.einsum('mxy,mtyz->mtxz', left_blocks, right_blocks, precision=lax.Pre...  21.3 us
    unnamed x1, blocking collectives  19.5 us
    all_gather x1, blocking collectives, local(): lax.all_gather(z_cols, 'row', axis=0, tiled=True)  19.2 us
    dot_general x1, matrix products, local(): summed = jnp.dot(matches, stacked, precision=lax.Precision.HIGHEST)  17 us
  transfers between devices with their start and end apart: 4, of which 3 were waited for; matrix products, arithmetic and copies ran while one was open for 2% of the time, Pallas kernels for 0%

commit v1 on v0

v1 whole, which is shorter than its diff:
```python
import functools

import jax
import jax.numpy as jnp
from jax import lax
from jax.experimental import pallas as pl
from jax.experimental.pallas import tpu as pltpu
from jax.sharding import Mesh
from jax.sharding import PartitionSpec as P

LANES = 128
SLOTS = (5, 6, 7, 8, 9, 10, 11, 12, 14, 16)
TOGETHER = 4
HBM = pl.BlockSpec(memory_space=pltpu.HBM)
ANY = pl.BlockSpec(memory_space=pl.ANY)
SMEM = pl.BlockSpec(memory_space=pltpu.SMEM)
VMEM = pl.BlockSpec(memory_space=pltpu.VMEM)


def sheet_kernel(panel, z_rows, z_cols, y_cols, sheet, *, per_cell):
    cols = panel.shape[0]
    got = panel[...].astype(jnp.float32)
    lane = lax.broadcasted_iota(jnp.int32, (LANES, LANES), 1)
    up = lax.broadcasted_iota(jnp.int32, (LANES, LANES), 0)
    cell = lax.broadcasted_iota(jnp.int32, (cols, LANES), 0)
    mine = cell == lax.broadcasted_iota(jnp.int32, (cols, LANES), 1) // per_cell
    lines = []
    for base in (0, per_cell):
        repeated = jnp.dot(
            got,
            (up == base + lane % per_cell).astype(jnp.float32),
            preferred_element_type=jnp.float32,
        )
        lines.append(jnp.sum(jnp.where(mine, repeated, 0.0), axis=0, keepdims=True))
    for v in (z_rows, z_cols, y_cols):
        v = v[...].astype(jnp.float32)
        lines.append(jnp.pad(v, ((0, 0), (0, LANES - v.shape[1]))))
    whole = jnp.concatenate(lines, axis=0).astype(jnp.int32)
    for r in range(sheet.shape[0]):
        sheet[r] = whole


def plan_kernel(
    where, info, plan, pick, spread, *, rows, cell_width, per_cell, group, half, targets, panel_rows
):
    shape = (rows, LANES)
    lane = lax.broadcasted_iota(jnp.int32, shape, 1)
    row = lax.broadcasted_iota(jnp.int32, shape, 0)
    x_row, x_col = info[:, 0, :], info[:, 1, :]
    z_code = info[:, 2, :] * cell_width + info[:, 3, :]
    y_col = info[:, 4, :].astype(jnp.float32)
    owner = lane // group
    inner = (lane // per_cell) % (group // per_cell) * cell_width + x_col
    spread[...] = lax.dot_general(
        y_col,
        (row == owner).astype(jnp.float32),
        (((0,), (0,)), ((), ())),
        preferred_element_type=jnp.float32,
    )
    met = jnp.zeros(shape, jnp.float32)
    for k in range(panel_rows):
        met = jnp.where(inner == k, spread[k : k + 1, :], met)
    code = x_row * cell_width + met.astype(jnp.int32)
    target = jnp.full(shape, -1, jnp.int32)
    first = lane
    for s in reversed(range(targets)):
        wanted = z_code[:, s : s + 1]
        target = jnp.where(code == wanted, s, target)
        first = jnp.where(z_code == wanted, s, first)
    used = target >= 0
    key = jnp.where(used, inner, -1 - lane)
    place = lane % group
    repeat = jnp.zeros(shape, jnp.int32)
    for d in range(1, group):
        same = (pltpu.roll(key, d, 1) == key) & (place >= d)
        repeat = jnp.where(same, d, repeat)
    sent = used & (repeat == 0)
    sent_f = sent.astype(jnp.float32)
    up = lax.broadcasted_iota(jnp.int32, (LANES, LANES), 0)
    across = lax.broadcasted_iota(jnp.int32, (LANES, LANES), 1)
    together = (up // group) == (across // group)
    before = (together & (up < across)).astype(jnp.float32)
    slot = jnp.dot(sent_f, before, preferred_element_type=jnp.float32).astype(jnp.int32)
    count = jnp.dot(sent_f, together.astype(jnp.float32), preferred_element_type=jnp.float32)
    held = slot
    for d in range(1, group):
        held = jnp.where(repeat == d, pltpu.roll(slot, d, 1), held)
    me, side = where[0], where[1]

    own_first = (LANES - group * me) % LANES
    mine = lambda v: pltpu.roll(v, own_first, 1)
    sent_slot, sent_row = mine(jnp.where(sent, slot, -1)), mine(inner)
    send = jnp.zeros(shape, jnp.int32)
    for t in range(group):
        send = jnp.where(lane == sent_slot[:, t : t + 1], sent_row[:, t : t + 1], send)
    plan[0] = send
    plan[1] = mine(count.astype(jnp.int32))

    def own(v):
        return jnp.sum(jnp.where(row == me, v.astype(jnp.float32), 0.0), axis=0, keepdims=True)

    used_f = used.astype(jnp.float32)
    rank = jnp.dot(used_f, (up < across).astype(jnp.float32), preferred_element_type=jnp.float32)
    chosen = (own(rank).astype(jnp.int32) == up) & (own(used_f) > 0.0)
    p = lane[:1]
    cell = p // per_cell
    facts = jnp.concatenate(
        [
            (cell % half * per_cell + p % per_cell).astype(jnp.float32),
            (cell // half == side).astype(jnp.float32),
            owner[:1].astype(jnp.float32),
            own(held),
            own(target),
            own(inner),
            jnp.zeros((2, LANES), jnp.float32),
        ]
    )
    listed = lax.dot_general(
        facts,
        chosen.astype(jnp.float32),
        (((1,), (1,)), ((), ())),
        preferred_element_type=jnp.float32,
    )
    total = jnp.sum(own(used_f), axis=1, keepdims=True)
    plan[2] = jnp.where(
        row == 6, total, jnp.where(row == 7, own(first), listed)
    ).astype(jnp.int32)
    most = jnp.max(jnp.where(owner == row, 0.0, count)).astype(jnp.int32)
    choice = jnp.int32(0)
    for limit in SLOTS[:-1]:
        choice = choice + (most > limit).astype(jnp.int32)
    pick[0] = choice


def pack_kernel(plan, where, y_blocks, out, sem, *, rows):
    me = where[0]
    started = jnp.int32(0)
    for r in range(rows):
        count = jnp.where(me == r, 0, plan[1, r, 0])

        @pl.loop(0, count)
        def _(j):
            pltpu.make_async_copy(y_blocks.at[plan[0, r, j]], out.at[r, j], sem).start()

        started = started + count

    @pl.loop(0, started)
    def _(_):
        pltpu.make_async_copy(y_blocks.at[0], out.at[0, 0], sem).wait()


X_PLACE, X_NEAR, OWNER, SLOT, TARGET, INNER, TOTAL, FIRST = range(8)


def unpack_kernel(plan, where, got, out, sem, *, group):
    me = where[0]

    def start(n, started):
        owner = plan[2, OWNER, n]

        @pl.when(owner != me)
        def _():
            pltpu.make_async_copy(got.at[owner, plan[2, SLOT, n]], out.at[n], sem).start()

        return started + (owner != me).astype(jnp.int32)

    started = lax.fori_loop(0, plan[2, TOTAL, 0], start, jnp.int32(0))

    @pl.loop(0, started)
    def _(_):
        pltpu.make_async_copy(got.at[0, 0], out.at[0], sem).wait()


def product_kernel(
    plan,
    where,
    x_near,
    x_far,
    y_blocks,
    y_lined,
    out,
    x_held,
    y_held,
    sums,
    into,
    x_sem,
    y_sem,
    out_sem,
    *,
    targets,
):
    me = where[0]
    total = plan[2, TOTAL, 0]

    @pl.loop(0, total)
    def _(n):
        place = plan[2, X_PLACE, n]
        near = plan[2, X_NEAR, n] > 0
        here = plan[2, OWNER, n] == me

        @pl.when(near)
        def _():
            pltpu.make_async_copy(x_near.at[place], x_held.at[n], x_sem.at[n]).start()

        @pl.when(jnp.logical_not(near))
        def _():
            pltpu.make_async_copy(x_far.at[place], x_held.at[n], x_sem.at[n]).start()

        @pl.when(here)
        def _():
            pltpu.make_async_copy(
                y_blocks.at[plan[2, INNER, n]], y_held.at[n], y_sem.at[n]
            ).start()

        @pl.when(jnp.logical_not(here))
        def _():
            pltpu.make_async_copy(y_lined.at[n], y_held.at[n], y_sem.at[n]).start()

        into[n] = plan[2, TARGET, n]

    for j in range(TOGETHER - 1):
        into[total + j] = targets
    sums[...] = jnp.zeros_like(sums)
    dot = functools.partial(jnp.dot, preferred_element_type=jnp.float32)

    @pl.loop(0, (total + TOGETHER - 1) // TOGETHER)
    def _(i):
        n = i * TOGETHER
        for j in range(TOGETHER):

            @pl.when(n + j < total)
            def _():
                pltpu.make_async_copy(x_near.at[0], x_held.at[n + j], x_sem.at[n + j]).wait()
                pltpu.make_async_copy(y_lined.at[0], y_held.at[n + j], y_sem.at[n + j]).wait()

        products = []
        for j in range(TOGETHER):
            x, y = x_held[n + j], y_held[n + j]
            x_hi, y_hi = x.astype(jnp.bfloat16), y.astype(jnp.bfloat16)
            x_lo = (x - x_hi.astype(jnp.float32)).astype(jnp.bfloat16)
            y_lo = (y - y_hi.astype(jnp.float32)).astype(jnp.bfloat16)
            products.append(
                dot(
                    jnp.concatenate([x_hi, x_lo, x_hi], axis=1),
                    jnp.concatenate([y_hi, y_hi, y_lo], axis=0),
                )
            )
        for j in range(TOGETHER):
            sums[into[n + j]] += products[j]

    for s in range(targets):
        pltpu.make_async_copy(sums.at[plan[2, FIRST, s]], out.at[s], out_sem).start()
    for s in range(targets):
        pltpu.make_async_copy(sums.at[0], out.at[s], out_sem).wait()


def local(x_blocks, x_rows, x_cols, y_blocks, y_cols, z_rows, z_cols):
    row_axes, col_axes = ("x", "y_hi"), ("y_lo", "z", "core")
    rows, cols = lax.axis_size(row_axes), lax.axis_size(col_axes)
    x_blocks = x_blocks[0]
    y_blocks = y_blocks[:, 0]
    per_cell, edge = x_blocks.shape[0], x_blocks.shape[-1]
    panel_rows = y_blocks.shape[0]
    targets = z_rows.shape[1]
    group = cols * per_cell // rows
    cell_width = panel_rows * rows // cols
    half = cols // 2
    me = lax.axis_index(row_axes)
    where = jnp.stack([me, lax.axis_index("y_lo")]).astype(jnp.int32)
    block = (edge, edge)

    across = lax.ppermute(x_blocks, "y_lo", [(0, 1), (1, 0)])
    x_near = lax.all_gather(x_blocks, ("z", "core"), axis=0, tiled=True)

    own = jnp.pad(jnp.concatenate([x_rows[0], x_cols[0]]), (0, LANES - 2 * per_cell))
    panel = lax.all_to_all(jnp.broadcast_to(own, (cols, 1, LANES)), col_axes, 0, 0, tiled=True)
    panel = panel.reshape(cols, LANES)
    across, panel = lax.optimization_barrier((across, panel))
    x_far = lax.all_gather(across, ("z", "core"), axis=0, tiled=True)
    sheet = pl.pallas_call(
        functools.partial(sheet_kernel, per_cell=per_cell),
        out_shape=jax.ShapeDtypeStruct((rows, 5, LANES), jnp.int32),
        in_specs=[VMEM] * 4,
        out_specs=VMEM,
        compiler_params=pltpu.CompilerParams(vmem_limit_bytes=4 * 2**20),
        name="sheet",
    )(panel, z_rows, z_cols, y_cols.reshape(1, panel_rows))
    info = lax.all_to_all(sheet, row_axes, 0, 0, tiled=True)

    plan, pick = pl.pallas_call(
        functools.partial(
            plan_kernel,
            rows=rows,
            cell_width=cell_width,
            per_cell=per_cell,
            group=group,
            half=half,
            targets=targets,
            panel_rows=panel_rows,
        ),
        out_shape=(
            jax.ShapeDtypeStruct((3, rows, LANES), jnp.int32),
            jax.ShapeDtypeStruct((1,), jnp.int32),
        ),
        in_specs=[SMEM, VMEM],
        out_specs=(VMEM, SMEM),
        scratch_shapes=[pltpu.VMEM((LANES, LANES), jnp.float32)],
        compiler_params=pltpu.CompilerParams(vmem_limit_bytes=4 * 2**20),
        name="plan",
    )(where, info)

    def with_slots(slots):
        def branch(plan, where, y_blocks):
            packed = pl.pallas_call(
                functools.partial(pack_kernel, rows=rows),
                out_shape=jax.ShapeDtypeStruct((rows, slots) + block, jnp.float32),
                in_specs=[SMEM, SMEM, HBM],
                out_specs=VMEM,
                scratch_shapes=[pltpu.SemaphoreType.DMA],
                compiler_params=pltpu.CompilerParams(vmem_limit_bytes=40 * 2**20),
                name="pack",
            )(plan, where, y_blocks)
            got = lax.all_to_all(packed, row_axes, 0, 0, tiled=True)
            return pl.pallas_call(
                functools.partial(unpack_kernel, group=group),
                out_shape=jax.ShapeDtypeStruct((LANES,) + block, jnp.float32),
                in_specs=[SMEM, SMEM, ANY],
                out_specs=HBM,
                scratch_shapes=[pltpu.SemaphoreType.DMA],
                compiler_params=pltpu.CompilerParams(vmem_limit_bytes=4 * 2**20),
                name="unpack",
            )(plan, where, got)

        return branch

    y_lined = lax.switch(pick[0], [with_slots(s) for s in SLOTS], plan, where, y_blocks)

    out = pl.pallas_call(
        functools.partial(product_kernel, targets=targets),
        out_shape=jax.ShapeDtypeStruct((targets,) + block, jnp.float32),
        in_specs=[SMEM, SMEM, HBM, HBM, HBM, HBM],
        out_specs=HBM,
        scratch_shapes=[
            pltpu.VMEM((LANES,) + block, jnp.float32),
            pltpu.VMEM((LANES,) + block, jnp.float32),
            pltpu.VMEM((targets + 1,) + block, jnp.float32),
            pltpu.SMEM((LANES + TOGETHER,), jnp.int32),
            pltpu.SemaphoreType.DMA((LANES,)),
            pltpu.SemaphoreType.DMA((LANES,)),
            pltpu.SemaphoreType.DMA,
        ],
        compiler_params=pltpu.CompilerParams(vmem_limit_bytes=60 * 2**20),
        name="products",
    )(plan, where, x_near, x_far, y_blocks, y_lined)
    return out[None]


def solution(mesh):
    chips = Mesh(mesh.devices.reshape(4, 2, 2, 8, 2), ("x", "y_hi", "y_lo", "z", "core"))
    row, col = ("x", "y_hi"), ("y_lo", "z", "core")
    flat, blocks = P(row, col), P(row, col, None, None)
    return jax.shard_map(
        local,
        mesh=chips,
        in_specs=(blocks, flat, flat, blocks, flat, flat, flat),
        out_specs=blocks,
        check_vma=False,
    )
```

time: 537 us -> 125 us (0.23)
  waiting for transfers between devices: 266 us -> 6.96 us
  blocking collectives: 175 us -> 74.9 us
  matrix products: 38.3 us -> 0 us
  local copies, waits for them, and re-layouts: 25.7 us -> 2.68 us
  Pallas kernels: 0 us -> 15.4 us
  starting transfers between devices: 14.5 us -> 9.05 us
    reduce_scatter x1 -> x0, waiting for transfers between devices: 229 us -> none  [local(): lax.psum_scatter(summed.reshape(targets * lax.axis_size('row'), block_edg...]
    all_gather x2 -> x0, blocking collectives: 146 us -> none  [the longest x1 126 us: local(): lax.all_gather(z_rows, 'row', axis=0, tiled=True)]
    all_to_all x1 -> x2, blocking collectives: 10 us -> 74.9 us  [the longest x1 57.9 us: branch(): got = lax.all_to_all(packed, row_axes, 0, 0, tiled=True)]
    dot_general x2 -> x0, matrix products: 38.3 us -> none  [the longest x1 21.3 us: local(): jnp.einsum('mxy,mtyz->mtxz', left_blocks, right_blocks, precision=lax.Pre...]
    all_gather x1 -> x2, waiting for transfers between devices: 30.4 us -> 0.04 us  [the longest x1 0.02 us: local(): x_near = lax.all_gather(x_blocks, ('z', 'core'), axis=0, tiled=True)]
    unnamed x1 -> x0, blocking collectives: 19.5 us -> none
    pallas_call x0 -> x5, Pallas kernels: none -> 15.4 us  [the longest x1 8.33 us: local(): pl.pallas_call(functools.partial(product_kernel, targets=targets), out_sh...]
    transpose x1 -> x0, local copies, waits for them, and re-layouts: 9.42 us -> none  [local(): jnp.einsum('mxy,mtyz->mtxz', left_blocks, right_blocks, precision=lax.Pre...]
  transfers between devices with their start and end apart: 4 -> 4, of which waited for: 3 -> 1; matrix products, arithmetic and copies ran while one was open for 2% -> 1% of each run, Pallas kernels for 0% -> 6%
where the time goes in v1:
time: 125 us; the launch traced here: 124 us
  blocking collectives  74.9 us (60%)
  Pallas kernels  15.4 us (12%)
  between operations  14.1 us (11%)
  starting transfers between devices  9.05 us (7%)
  waiting for transfers between devices  6.96 us (6%)
  local copies, waits for them, and re-layouts  2.68 us (2%)
    all_to_all x1, blocking collectives, branch(): got = lax.all_to_all(packed, row_axes, 0, 0, tiled=True)  57.9 us
    all_to_all x1, blocking collectives, local(): lax.all_to_all(jnp.broadcast_to(own, (cols, 1, LANES)), col_axes, 0, 0, t...  17.1 us
    pallas_call x1, Pallas kernels, local(): pl.pallas_call(functools.partial(product_kernel, targets=targets), out_sh...  8.33 us
    all_to_all x1, starting transfers between devices, local(): info = lax.all_to_all(sheet, row_axes, 0, 0, tiled=True)  7.35 us
    all_to_all x1, waiting for transfers between devices, local(): info = lax.all_to_all(sheet, row_axes, 0, 0, tiled=True)  6.19 us
    unnamed x8, local copies, waits for them, and re-layouts  2.66 us
  transfers between devices with their start and end apart: 4, of which 1 were waited for; matrix products, arithmetic and copies ran while one was open for 1% of the time, Pallas kernels for 6%

profile of v1, /device:TPU:2, one launch (start us, length us, event | category | flops | bytes accessed | tf_op | source)
XLA Modules:
  0.0 124.0 jit_solution(2352740214517505415)
XLA Ops:
  6.5 0.0 all-gather.6.cloned.1.call-start
  6.5 0.7 all-gather.6.cloned.1.call-update
  7.3 0.0 all-gather.4.cloned.1.call-start
  7.3 1.7 %collective-permute-start = (f32[4,128,128]{2,1,0:T(8,128)}, f32[4,128,128]{2,1,0:T(8,128)S(1)}, u32[]{:S(2)}, u32[]{:S(2)}) collective-permute-start(f32[4,128,128]{2,1,0:T(8,128)} %bitcast.27), channel_id=1, source_target_pairs={{0,16},{16,0},{1,17},{17,1},{2,18},{18,2},{3,19},{19,3},{4,20},{20... | collective-permute-start | bytes 786440 | tf_op jit(solution)/shard_map/ppermute | solution.py:272
  9.0 0.7 pad_add_fusion.1
  9.7 17.1 %all_to_all.60 = s32[32,1,128]{2,1,0:T(1,128)S(1)} all-to-all(s32[32,1,128]{2,1,0:T(1,128)S(1)} %broadcast_in_dim.6), channel_id=1, replica_groups=mesh['x'=4,'y_hi'=2,'y_lo'=2,'z'=8,'core'=2] {'y_lo','z','core'}, dimensions={0} | all-to-all | bytes 32768 | tf_op jit(solution)/shard_map/all_to_all | solution.py:276
  26.8 0.0 collective-permute-done
  26.8 0.0 copy-start.3
  26.8 0.7 copy-done.3
  27.5 0.0 all-gather.4.cloned.1.call-update
  27.5 0.0 copy-start
  27.5 0.6 copy-done
  28.2 0.0 copy-start.1
  28.2 0.7 copy-done.1
  28.8 0.0 copy-start.2
  28.8 0.7 copy-done.2
  29.5 0.8 sheet.1
  30.3 7.3 %all-to-all-start.11 = ((s32[8,5,128]{2,1,0:T(8,128)}), s32[8,5,128]{2,1,0:T(8,128)S(1)}, u32[]{:S(2)}, u32[]{:S(2)}) async-start(s32[8,5,128]{2,1,0:T(8,128)} %sheet.1), calls=%async_computation.11 | async-start | bytes 65536 | tf_op jit(solution)/shard_map/all_to_all | solution.py:288
  37.6 0.1 pad_add_fusion.where
  37.7 6.2 %all-to-all-done.11.info = s32[8,5,128]{2,1,0:T(8,128)S(1)} async-done(((s32[8,5,128]{2,1,0:T(8,128)}), s32[8,5,128]{2,1,0:T(8,128)S(1)}, u32[]{:S(2)}, u32[]{:S(2)}) %all-to-all-start.11) | async-done | bytes 20512 | tf_op jit(solution)/shard_map/all_to_all | solution.py:288
  43.9 2.0 %plan.1 = (s32[3,8,128]{2,1,0:T(8,128)S(1)}, s32[1]{0:T(128)}) custom-call(s32[2]{0:T(128)S(1)} %pad_add_fusion.where, s32[8,5,128]{2,1,0:T(8,128)S(1)} %all-to-all-done.11.info), custom_call_target="tpu_custom_call" | custom-call | tf_op jit(solution)/shard_map/plan/pallas_call | solution.py:290
  46.5 62.3 %conditional.1 = (f32[128,128,128]{2,1,0:T(8,128)}) conditional(s32[]{:T(128)} %bitcast.10, (s32[3,8,128]{2,1,0:T(8,128)S(1)}, s32[2]{0:T(128)S(1)}, f32[76,128,128]{2,1,0:T(8,128)}) %tuple.52, (s32[3,8,128]{2,1,0:T(8,128)S(1)}, s32[2]{0:T(128)S(1)}, f32[76,128,128]{2,1,0:T(8,128)}) %tuple.53, ...), branch_computations={%region_0.1_spmd, %region_1.2_spmd, %region_2.3_spmd, %region_3.4_... | conditional | bytes 16777224 | solution.py:336
  46.6 2.2 %pack.14 = f32[8,9,128,128]{3,2,1,0:T(8,128)S(1)} custom-call(s32[3,8,128]{2,1,0:T(8,128)S(1)} %get-tuple-element.88.plan, s32[2]{0:T(128)S(1)} %get-tuple-element.89.where, f32[76,128,128]{2,1,0:T(8,128)} %get-tuple-element.90.y_blocks), custom_call_target="tpu_custom_call" | custom-call | tf_op jit(solution)/shard_map/cond/branch_4_fun/pack/pallas_call | solution.py:314
  48.8 57.9 %all_to_all.54.got = f32[8,9,128,128]{3,2,1,0:T(8,128)S(1)} all-to-all(f32[8,9,128,128]{3,2,1,0:T(8,128)S(1)} %pack.14), channel_id=1, replica_groups=mesh['x'=4,'y_hi'=2,'y_lo'=2,'z'=8,'core'=2] {'x','y_hi'}, dimensions={0} | all-to-all | bytes 9437184 | tf_op jit(solution)/shard_map/cond/branch_4_fun/all_to_all | solution.py:323
  106.7 2.1 %unpack.14 = f32[128,128,128]{2,1,0:T(8,128)} custom-call(s32[3,8,128]{2,1,0:T(8,128)S(1)} %get-tuple-element.88.plan, s32[2]{0:T(128)S(1)} %get-tuple-element.89.where, f32[8,9,128,128]{3,2,1,0:T(8,128)S(1)} %all_to_all.54.got), custom_call_target="tpu_custom_call" | custom-call | tf_op jit(solution)/shard_map/cond/branch_4_fun/unpack/pallas_call | solution.py:324
  108.8 0.0 all-gather.6.cloned.1.call-done
  108.8 0.0 all-gather.4.cloned.1.call-done.x_far
  108.9 8.3 %products.1 = f32[40,128,128]{2,1,0:T(8,128)} custom-call(s32[3,8,128]{2,1,0:T(8,128)S(1)} %get-tuple-element.111.plan, s32[2]{0:T(128)S(1)} %pad_add_fusion.where, f32[64,128,128]{2,1,0:T(8,128)} %bitcast.25, f32[64,128,128]{2,1,0:T(8,128)} %all-gather.4.cloned.1.call-done.x_far, f32[76,128,128]{2,1,0:T(8,128)} %bitcast.24, ...), custom_call_target="tpu_custom_call" | custom-call | tf_op jit(solution)/shard_map/products/pallas_call | solution.py:338
  (2 shorter events, 0.0 us)
Async XLA Ops:
  6.5 102.3 %all-gather.6.cloned.1.call-start = ((), (), s32[]{:S(2)}) async-start(), calls=%async_computation.13 | async-start | bytes 4456448 | tf_op jit(solution)/shard_map/all_gather | solution.py:273
  7.3 101.6 %all-gather.4.cloned.1.call-start = ((), (), s32[]{:S(2)}) async-start(), calls=%async_computation.12 | async-start | bytes 4456448 | tf_op jit(solution)/shard_map/all_gather | solution.py:279
  7.3 19.5 %collective-permute-start = (f32[4,128,128]{2,1,0:T(8,128)}, f32[4,128,128]{2,1,0:T(8,128)S(1)}, u32[]{:S(2)}, u32[]{:S(2)}) collective-permute-start(f32[4,128,128]{2,1,0:T(8,128)} %bitcast.27), channel_id=1, source_target_pairs={{0,16},{16,0},{1,17},{17,1},{2,18},{18,2},{3,19},{19,3},{4,20},{20... | collective-permute-start | bytes 786440 | tf_op jit(solution)/shard_map/ppermute | solution.py:272
  26.8 0.7 copy-start.3
  27.5 0.7 copy-start
  28.2 0.7 copy-start.1
  28.8 0.7 copy-start.2
  30.3 13.6 %all-to-all-start.11 = ((s32[8,5,128]{2,1,0:T(8,128)}), s32[8,5,128]{2,1,0:T(8,128)S(1)}, u32[]{:S(2)}, u32[]{:S(2)}) async-start(s32[8,5,128]{2,1,0:T(8,128)} %sheet.1), calls=%async_computation.11 | async-start | bytes 65536 | tf_op jit(solution)/shard_map/all_to_all | solution.py:288
Sparse Core Ops, SparseCore 0:
  9.2 45.0 all-gather.5
  56.1 40.9 all-gather.3
